TPU v7x, 128 devices: a whole 4x4x4 slice. The times are simulated.
128 devices in a mesh: str: 16 (over x_lo, y, core), crs: 8 (over x_hi, z).
Axes of the slice: x: 4 (x_hi: 2, x_lo: 2; x = x_hi * 2 + x_lo), y: 4, z: 4, core: 2. Of those that a mesh axis runs over, the one named last changes fastest.
Arguments:
- voltage: float32 [4, 512, 16384], P(None, 'str', 'crs'), may hold values from -4 to 0.5
- photocurrent: float32 [4, 512, 16384], P(None, 'str', 'crs'), may hold values from 0.1 to 10
- shunt: float32 [512, 16384], P('str', 'crs'), may hold values from 0.02 to 0.5
- series: float32 [512, 16384], P('str', 'crs'), may hold values from 0.5 to 2
- pattern: int32 [512, 128], P('str', 'crs'), may hold values from 0 to 3
- diode_mask: int32 [512, 128], P('str', 'crs'), may hold values 0 or 1
- aggregate: int32 [512, 128], P('str', 'crs'), may hold values from 0 to 4095, as said below
- coarse_inverse: float32 [4096, 4096], P('crs'), as said below
Outputs:
- newton_step: float32 [4, 512, 16384], P(None, 'str', 'crs')
- residual: float32 [4, 512, 16384], P(None, 'str', 'crs')
Inputs may be any that keep to these rules, and one draw needn't show every extreme that they name: `aggregate`: every value appears. coarse_inverse is symmetric positive definite.
All inputs are finite; a program needn't handle non-finite values. No bound on the sum of `diode_mask` on one device may be relied on, other than what follows from the above.
Results may differ from a plain program's by a relative error of at most 0.0003.
Values sent between devices are 32-bit elements; how exact they have to be, the bound alone decides.
A program may use at most 64 MiB of HBM per device.

v0:
```python
import jax
import jax.numpy as jnp
from jax import lax
from jax.sharding import PartitionSpec as P

ITERS = 3
LEVELS = (0.25, 0.5, 1.0, 2.0)
DIODE_SAT = 0.5


def with_halo(block, sides, width, periodic):
    for axis, dim in sides:
        count = lax.axis_size(axis)
        forward = [(i, i + 1) for i in range(count - 1)]
        if periodic:
            forward.append((count - 1, 0))
        backward = [(target, source) for source, target in forward]
        low = lax.ppermute(
            lax.slice_in_dim(block, block.shape[dim] - width, None, axis=dim), axis, forward
        )
        high = lax.ppermute(lax.slice_in_dim(block, 0, width, axis=dim), axis, backward)
        block = jnp.concatenate([low, block, high], axis=dim)
    return block


def widen(blocks):
    shape = blocks.shape
    spread = jnp.broadcast_to(blocks[..., None], shape + (128,))
    return spread.reshape(shape[:-1] + (shape[-1] * 128,))


def cross_levels(pattern):
    total = jnp.zeros(pattern.shape, jnp.float32)
    for number in range(4):
        total = total + jnp.where(pattern == number, jnp.float32(LEVELS[number]), jnp.float32(0.0))
    return total


def neighbours(field):
    along = with_halo(field, (("str", 1),), 1, True)
    across = with_halo(field, (("crs", 2),), 1, False)
    return (along[:, 2:], along[:, :-2], across[:, :, 2:], across[:, :, :-2])


def shards(voltage, photocurrent, shunt, series, pattern, diode_mask, aggregate, coarse_inverse):
    points = voltage.shape[0]
    rows_here = voltage.shape[1]
    local_block_list = voltage.shape[2] // 128
    coarse_count = coarse_inverse.shape[1]
    cross_level = widen(cross_levels(pattern))
    diode_area = widen(diode_mask.astype(jnp.float32))
    flat_groups = aggregate.reshape(-1)
    stacked = jnp.concatenate([voltage, cross_level[None], series[None]], axis=0)
    below, above, right_cells, left_cells = neighbours(stacked)
    right_link = jnp.minimum(cross_level, right_cells[points])
    left_link = jnp.minimum(cross_level, left_cells[points])
    up_link = above[points + 1]
    diode_derivative = DIODE_SAT * diode_area * jnp.exp(voltage)
    imbalance = (
        shunt * voltage
        + series * (voltage - below[:points])
        + up_link * (voltage - above[:points])
        + right_link * (voltage - right_cells[:points])
        + left_link * (voltage - left_cells[:points])
        + diode_derivative
        - DIODE_SAT * diode_area
        - photocurrent
    )
    diagonal = shunt + diode_derivative + series + up_link + right_link + left_link

    def restrict(remainder):
        block_sums = remainder.reshape(points, rows_here * local_block_list, 128).sum(axis=-1)
        return jax.ops.segment_sum(block_sums.T, flat_groups, num_segments=coarse_count).T

    def interpolate_upward(correction):
        picked = jnp.take(correction, flat_groups, axis=1)
        return widen(picked.reshape(points, rows_here, local_block_list))

    def coarse_solve(incomplete_value):
        product = None
        total = lax.psum(incomplete_value, ("str", "crs"))
        row_share = lax.dot_general(
            total, coarse_inverse, (((1,), (1,)), ((), ())), precision=lax.Precision.HIGHEST
        )
        correction = lax.all_gather(row_share, "crs", axis=1, tiled=True)
        return (correction, product)

    def precondition(remainder):
        resident_portion = remainder / diagonal
        incomplete_value = restrict(remainder)
        correction, product = coarse_solve(incomplete_value)
        smoothed = resident_portion + interpolate_upward(correction)
        product = lax.psum(jnp.sum(remainder * smoothed, axis=(1, 2)), ("str", "crs"))
        return (smoothed, product)

    remainder = -imbalance
    newton_step = jnp.zeros_like(voltage)
    smoothed, product = precondition(remainder)
    direction = smoothed
    for turn in range(ITERS):
        operate_below, operate_above, operate_right_cells, operate_left_cells = neighbours(
            direction
        )
        image = (
            diagonal * direction
            - series * operate_below
            - up_link * operate_above
            - right_link * operate_right_cells
            - left_link * operate_left_cells
        )
        curvature = lax.psum(jnp.sum(direction * image, axis=(1, 2)), ("str", "crs"))
        alpha = (product / curvature)[:, None, None]
        newton_step = newton_step + alpha * direction
        remainder = remainder - alpha * image
        if turn + 1 < ITERS:
            smoothed, fresh = precondition(remainder)
            ratio = (fresh / product)[:, None, None]
            direction = smoothed + ratio * direction
            product = fresh
    return (newton_step, remainder)


def solution(mesh):
    placed = (
        P(None, "str", "crs"),
        P(None, "str", "crs"),
        P("str", "crs"),
        P("str", "crs"),
        P("str", "crs"),
        P("str", "crs"),
        P("str", "crs"),
        P("crs", None),
    )
    return jax.shard_map(
        shards,
        mesh=mesh,
        in_specs=placed,
        out_specs=(P(None, "str", "crs"), P(None, "str", "crs")),
        check_vma=False,
    )
```

profile of v0, /device:TPU:1, one launch (start us, length us, event | category | flops | bytes accessed | tf_op | source)
XLA Modules:
  0.0 1062.8 jit_solution(3380685636923150555)
XLA Ops:
  9.5 1.5 collective-permute-start
  11.0 1.3 collective-permute-start.1
  13.7 4.2 collective-permute-start.3
  20.6 2.9 fusion.30
  24.8 1.6 reduce_sum.81
  26.5 3.8 scatter_custom_fusion
  30.4 158.7 %all-reduce.5.cloned.1.call-done = f32[4,4096]{0,1:T(8,128)} async-done(((f32[4,4096]{0,1:T(8,128)}), f32[4,4096]{0,1:T(8,128)}) %all-reduce.5.cloned.1.call-update) | async-done | bytes 65552 | tf_op jit(solution)/shard_map/psum | solution.py:81
  189.0 10.9 %fusion.54 = f32[4,512]{1,0:T(4,128)S(1)} fusion(f32[4,4096]{0,1:T(8,128)} %all-reduce.5.cloned.1.call-done, f32[512,4096]{1,0:T(8,128)} %param.17), kind=kOutput, calls=%fused_computation.118 | convolution fusion | flops 100663296 | bytes 8462336 | tf_op jit(solution)/shard_map/dot_general | solution.py:82
  199.9 28.1 %all_gather.9 = f32[4,4096]{1,0:T(4,128)S(1)} all-gather(f32[4,512]{1,0:T(4,128)S(1)} %fusion.54), channel_id=1, replica_groups=mesh['str'=16,'crs'=8] {'crs'}, dimensions={1}, use_global_device_ids=true | all-gather | bytes 73728 | tf_op jit(solution)/shard_map/all_gather | solution.py:85
  228.7 1.6 gather_fusion
  233.2 2.6 divide_add_fusion.2
  235.8 7.2 collective-permute-start.4
  245.6 4.0 collective-permute-start.7
  249.7 1.8 collective-permute-done.7
  252.5 69.2 %all-reduce = (f32[4]{0:T(128)}, f32[4]{0:T(128)}) all-reduce(f32[4]{0:T(128)S(1)} %get-tuple-element.4, f32[4]{0:T(128)S(1)} %get-tuple-element.3), channel_id=1, replica_groups=mesh['str'=16,'crs'=8] {'str','crs'}, use_global_device_ids=true, to_apply=%region_4.6 | all-reduce | flops 8 | bytes 64 | tf_op jit(solution)/shard_map/psum | solution.py:93
  322.4 2.8 multiply_subtract_fusion.2
  325.2 1.4 reshape.56
  327.1 3.8 scatter_custom_fusion.1
  331.1 147.5 %all-reduce.7.cloned.1.call-done = f32[4,4096]{0,1:T(8,128)} async-done(((f32[4,4096]{0,1:T(8,128)}), f32[4,4096]{0,1:T(8,128)}) %all-reduce.7.cloned.1.call-update) | async-done | bytes 65552 | tf_op jit(solution)/shard_map/psum | solution.py:81
  478.6 10.9 %fusion.55 = f32[4,512]{1,0:T(4,128)S(1)} fusion(f32[4,4096]{0,1:T(8,128)} %all-reduce.7.cloned.1.call-done, f32[512,4096]{1,0:T(8,128)} %param.17), kind=kOutput, calls=%fused_computation.119 | convolution fusion | flops 100663296 | bytes 8462336 | tf_op jit(solution)/shard_map/dot_general | solution.py:82
  489.4 27.8 %all_gather.10 = f32[4,4096]{1,0:T(4,128)S(1)} all-gather(f32[4,512]{1,0:T(4,128)S(1)} %fusion.55), channel_id=1, replica_groups=mesh['str'=16,'crs'=8] {'crs'}, dimensions={1}, use_global_device_ids=true | all-gather | bytes 73728 | tf_op jit(solution)/shard_map/all_gather | solution.py:85
  517.2 2.0 copy.34
  519.2 3.3 gather_fusion.1
  522.6 1.8 broadcast_select_fusion.1
  526.9 2.4 reshape.57
  529.3 1.6 multiply_reduce_fusion.3
  530.8 70.0 %psum.67 = f32[4]{0:T(128)S(1)} all-reduce(f32[4]{0:T(128)S(1)} %multiply_reduce_fusion.3), channel_id=1, replica_groups=mesh['str'=16,'crs'=8] {'str','crs'}, use_global_device_ids=true, to_apply=%region_11.13 | all-reduce | flops 4 | bytes 32 | tf_op jit(solution)/shard_map/psum | solution.py:93
  600.8 1.9 multiply_add_fusion.2
  606.0 4.0 collective-permute-start.11
  613.3 71.4 %psum.68 = f32[4]{0:T(128)} all-reduce(f32[4]{0:T(128)S(1)} %multiply_reduce_fusion.2), channel_id=1, replica_groups=mesh['str'=16,'crs'=8] {'str','crs'}, use_global_device_ids=true, to_apply=%region_13.15 | all-reduce | flops 4 | bytes 32 | tf_op jit(solution)/shard_map/psum | solution.py:111
  685.4 3.1 multiply_subtract_fusion.1
  688.5 2.4 reshape.58
  690.8 1.6 reduce_sum.87
  693.3 4.1 scatter_custom_fusion.2
  697.3 147.4 %all-reduce.9.cloned.1.call-done = f32[4,4096]{0,1:T(8,128)} async-done(((f32[4,4096]{0,1:T(8,128)}), f32[4,4096]{0,1:T(8,128)}) %all-reduce.9.cloned.1.call-update) | async-done | bytes 65552 | tf_op jit(solution)/shard_map/psum | solution.py:81
  844.8 10.9 %fusion.56 = f32[4,512]{1,0:T(4,128)S(1)} fusion(f32[4,4096]{0,1:T(8,128)} %all-reduce.9.cloned.1.call-done, f32[512,4096]{1,0:T(8,128)} %param.17), kind=kOutput, calls=%fused_computation.120 | convolution fusion | flops 100663296 | bytes 8462336 | tf_op jit(solution)/shard_map/dot_general | solution.py:82
  855.6 27.8 %all_gather.11 = f32[4,4096]{1,0:T(4,128)S(1)} all-gather(f32[4,512]{1,0:T(4,128)S(1)} %fusion.56), channel_id=1, replica_groups=mesh['str'=16,'crs'=8] {'crs'}, dimensions={1}, use_global_device_ids=true | all-gather | bytes 73728 | tf_op jit(solution)/shard_map/all_gather | solution.py:85
  883.4 2.0 copy.37
  885.4 3.2 gather_fusion.2
  888.6 1.8 broadcast_select_fusion
  893.0 2.4 reshape.59
  895.4 1.9 multiply_reduce_fusion.1
  897.2 70.1 %psum.70 = f32[4]{0:T(128)S(1)} all-reduce(f32[4]{0:T(128)S(1)} %multiply_reduce_fusion.1), channel_id=1, replica_groups=mesh['str'=16,'crs'=8] {'str','crs'}, use_global_device_ids=true, to_apply=%region_18.20 | all-reduce | flops 4 | bytes 32 | tf_op jit(solution)/shard_map/psum | solution.py:93
  967.4 1.9 multiply_add_fusion.1
  972.6 4.0 collective-permute-start.15
  979.9 71.0 %psum.71 = f32[4]{0:T(128)} all-reduce(f32[4]{0:T(128)S(1)} %multiply_reduce_fusion), channel_id=1, replica_groups=mesh['str'=16,'crs'=8] {'str','crs'}, use_global_device_ids=true, to_apply=%region_20.22 | all-reduce | flops 4 | bytes 32 | tf_op jit(solution)/shard_map/psum | solution.py:111
  1051.6 2.7 multiply_add_fusion
  1054.3 1.7 multiply_subtract_fusion
  (160 shorter events, 36.8 us)
Async XLA Ops:
  7.2 5.2 copy-start.1
  7.2 5.1 copy-start
  7.2 181.9 %all-reduce.5.cloned.1.call-start = ((), (), s32[]{:S(2)}) async-start(), calls=%async_computation | async-start | bytes 4194304 | tf_op jit(solution)/shard_map/psum | solution.py:81
  8.1 9.8 copy-start.39
  8.1 9.8 copy-start.37
  9.5 10.3 collective-permute-start
  11.0 8.6 collective-permute-start.1
  12.4 7.1 collective-permute-start.2
  13.7 5.8 collective-permute-start.3
  19.8 3.7 copy-start.7
  19.8 3.7 copy-start.12
  19.8 3.7 copy-start.17
  23.5 6.8 copy-start.3
  26.5 3.9 copy-start.38
  30.3 448.3 %all-reduce.7.cloned.1.call-start = ((), (), s32[]{:S(2)}) async-start(), calls=%async_computation.1 | async-start | bytes 4194304 | tf_op jit(solution)/shard_map/psum | solution.py:81
  199.9 30.4 %copy-start.36 = (pred[512]{0:T(512)(128)(4,1)S(1)}, pred[512]{0:T(512)(128)(4,1)}, u32[]{:S(2)}) copy-start(pred[512]{0:T(512)(128)(4,1)} %compare_and_fusion) | copy-start | bytes 1540
  233.2 18.4 %copy-start.4 = (f32[4,32,2048]{2,1,0:T(8,128)S(1)}, f32[4,32,2048]{2,1,0:T(8,128)}, u32[]{:S(2)}) copy-start(f32[4,32,2048]{2,1,0:T(8,128)} %copy-done.3) | copy-start | bytes 3145732
  233.2 18.4 %copy-start.8 = (f32[32,2048]{1,0:T(8,128)S(1)}, f32[32,2048]{1,0:T(8,128)}, u32[]{:S(2)}) copy-start(f32[32,2048]{1,0:T(8,128)} %copy-done.7) | copy-start | bytes 786436
  233.2 18.4 %copy-start.13 = (f32[32,2048]{1,0:T(8,128)S(1)}, f32[32,2048]{1,0:T(8,128)}, u32[]{:S(2)}) copy-start(f32[32,2048]{1,0:T(8,128)} %copy-done.12) | copy-start | bytes 786436
  233.2 18.4 %copy-start.18 = (f32[32,2048]{1,0:T(8,128)S(1)}, f32[32,2048]{1,0:T(8,128)}, u32[]{:S(2)}) copy-start(f32[32,2048]{1,0:T(8,128)} %copy-done.17) | copy-start | bytes 786436
  235.8 15.7 %collective-permute-start.4 = (f32[4,1,2048]{2,1,0:T(1,128)S(1)}, f32[4,1,2048]{2,1,0:T(1,128)S(1)}, u32[]{:S(2)}, u32[]{:S(2)}) collective-permute-start(f32[4,1,2048]{2,1,0:T(1,128)S(1)} %get-tuple-element.24), channel_id=1, source_target_pairs={{8,0},{16,8},{24,16},{32,24},{40,32},{48,40},{56,48},{64,56},{72,6... | collective-permute-start | bytes 98312 | tf_op jit(solution)/shard_map/ppermute | solution.py:21
  243.0 8.6 collective-permute-start.5
  244.3 5.4 collective-permute-start.6
  245.6 5.9 collective-permute-start.7
  251.6 70.8 %copy-start.5 = (f32[4,32,2048]{2,1,0:T(8,128)S(1)}, f32[4,32,2048]{2,1,0:T(8,128)}, u32[]{:S(2)}) copy-start(f32[4,32,2048]{2,1,0:T(8,128)} %copy-done.3) | copy-start | bytes 3145732
  330.9 513.9 %all-reduce.9.cloned.1.call-start = ((), (), s32[]{:S(2)}) async-start(), calls=%async_computation.2 | async-start | bytes 4194304 | tf_op jit(solution)/shard_map/psum | solution.py:81
  519.2 10.0 copy-start.6
  529.3 71.5 %copy-start.42 = (f32[4]{0:T(128)S(1)}, f32[4]{0:T(128)}, u32[]{:S(2)}) copy-start(f32[4]{0:T(128)} %get-tuple-element.5) | copy-start | bytes 52
  600.8 11.7 %copy-start.9 = (f32[32,2048]{1,0:T(8,128)S(1)}, f32[32,2048]{1,0:T(8,128)}, u32[]{:S(2)}) copy-start(f32[32,2048]{1,0:T(8,128)} %copy-done.7) | copy-start | bytes 786436
  600.8 11.7 %copy-start.14 = (f32[32,2048]{1,0:T(8,128)S(1)}, f32[32,2048]{1,0:T(8,128)}, u32[]{:S(2)}) copy-start(f32[32,2048]{1,0:T(8,128)} %copy-done.12) | copy-start | bytes 786436
  600.8 11.7 %copy-start.19 = (f32[32,2048]{1,0:T(8,128)S(1)}, f32[32,2048]{1,0:T(8,128)}, u32[]{:S(2)}) copy-start(f32[32,2048]{1,0:T(8,128)} %copy-done.17) | copy-start | bytes 786436
  602.8 8.5 collective-permute-start.8
  604.0 7.3 collective-permute-start.9
  604.7 5.7 collective-permute-start.10
  606.0 5.3 collective-permute-start.11
  895.4 72.0 %copy-start.41 = (f32[4]{0:T(128)S(1)}, f32[4]{0:T(128)}, u32[]{:S(2)}) copy-start(f32[4]{0:T(128)} %copy-done.40) | copy-start | bytes 52
  967.4 11.7 %copy-start.10 = (f32[32,2048]{1,0:T(8,128)S(1)}, f32[32,2048]{1,0:T(8,128)}, u32[]{:S(2)}) copy-start(f32[32,2048]{1,0:T(8,128)} %copy-done.7) | copy-start | bytes 786436
  967.4 11.7 %copy-start.15 = (f32[32,2048]{1,0:T(8,128)S(1)}, f32[32,2048]{1,0:T(8,128)}, u32[]{:S(2)}) copy-start(f32[32,2048]{1,0:T(8,128)} %copy-done.12) | copy-start | bytes 786436
  967.4 11.7 %copy-start.20 = (f32[32,2048]{1,0:T(8,128)S(1)}, f32[32,2048]{1,0:T(8,128)}, u32[]{:S(2)}) copy-start(f32[32,2048]{1,0:T(8,128)} %copy-done.17) | copy-start | bytes 786436
  969.3 8.6 copy-start.22
  969.4 8.5 collective-permute-start.12
  970.5 7.3 collective-permute-start.13
  971.3 5.7 collective-permute-start.14
  972.6 5.3 collective-permute-start.15
  1051.6 2.7 copy-start.21
  1051.6 2.7 copy-start.23
  1051.6 2.7 copy-start.27
  1051.6 2.7 copy-start.30
  (14 other events, 17.6 us)
Sparse Core Ops, SparseCore 0:
  30.4 158.5 all-reduce.4
  331.0 147.5 all-reduce.6
  697.5 147.2 all-reduce.8
where the time goes:
time: 1070 us; the launch traced here: 1060 us
  waiting for transfers between devices  458 us (43%)
  blocking collectives  435 us (41%)
  other arithmetic  50.6 us (5%)
  starting transfers between devices  36.5 us (3%)
  local copies, waits for them, and re-layouts  35 us (3%)
  matrix products  32.6 us (3%)
  between operations  14.5 us (1%)
    psum x3, waiting for transfers between devices, coarse_solve(): total = lax.psum(incomplete_value, ('str', 'crs'))  454 us
    psum x3, blocking collectives, precondition(): lax.psum(jnp.sum(remainder * smoothed, axis=(1, 2)), ('str', 'crs'))  209 us
    psum x2, blocking collectives, shards(): lax.psum(jnp.sum(direction * image, axis=(1, 2)), ('str', 'crs'))  142 us
    all_gather x3, blocking collectives, coarse_solve(): correction = lax.all_gather(row_share, 'crs', axis=1, tiled=True)  83.8 us
    dot_general x3, matrix products, coarse_solve(): lax.dot_general(total, coarse_inverse, (((1,), (1,)), ((), ())), precisio...  32.6 us
  transfers between devices with their start and end apart: 19, of which 9 were waited for; matrix products, arithmetic and copies ran while one was open for 0% of the time, Pallas kernels for 0%

commit v1 on v0

--- a/solution.py
+++ b/solution.py
@@ -1,3 +1,4 @@
+import functools
 import jax
 import jax.numpy as jnp
 from jax import lax
@@ -6,6 +7,15 @@
 ITERS = 3
 LEVELS = (0.25, 0.5, 1.0, 2.0)
 DIODE_SAT = 0.5
+
+
+def regions_tell(x0, where_dim):
+    return jnp.concatenate(
+        lax.all_to_all(jnp.stack([x0] * lax.axis_size("crs")), "crs", 0, 0), axis=where_dim
+    )
+
+
+step_on_the_tracks = functools.partial(regions_tell, where_dim=1)
 
 
 def with_halo(block, sides, width, periodic):
@@ -82,7 +92,7 @@
         row_share = lax.dot_general(
             total, coarse_inverse, (((1,), (1,)), ((), ())), precision=lax.Precision.HIGHEST
         )
-        correction = lax.all_gather(row_share, "crs", axis=1, tiled=True)
+        correction = step_on_the_tracks(row_share)
         return (correction, product)
 
     def precondition(remainder):

time: 1070 us -> 1010 us (0.944)
  blocking collectives: 435 us -> 365 us
    all_gather x3 -> x0, blocking collectives: 83.8 us -> none  [coarse_solve(): correction = lax.all_gather(row_share, 'crs', axis=1, tiled=True)]
    all_to_all x0 -> x2, blocking collectives: none -> 23.6 us  [regions_tell(): lax.all_to_all(jnp.stack([x0] * lax.axis_size('crs')), 'crs', 0, 0)]
  transfers between devices with their start and end apart: 19 -> 20, of which waited for: 9 -> 10; matrix products, arithmetic and copies ran while one was open for 0% -> 0% of each run, Pallas kernels for 0% -> 0%
where the time goes in v1:
time: 1010 us; the launch traced here: 998 us
  waiting for transfers between devices  464 us (46%)
  blocking collectives  365 us (36%)
  other arithmetic  50.9 us (5%)
  local copies, waits for them, and re-layouts  36.8 us (4%)
  starting transfers between devices  35.4 us (4%)
  matrix products  32.6 us (3%)
  between operations  14.6 us (1%)
    psum x3, waiting for transfers between devices, coarse_solve(): total = lax.psum(incomplete_value, ('str', 'crs'))  453 us
    psum x3, blocking collectives, precondition(): lax.psum(jnp.sum(remainder * smoothed, axis=(1, 2)), ('str', 'crs'))  199 us
    psum x2, blocking collectives, shards(): lax.psum(jnp.sum(direction * image, axis=(1, 2)), ('str', 'crs'))  142 us
    dot_general x3, matrix products, coarse_solve(): lax.dot_general(total, coarse_inverse, (((1,), (1,)), ((), ())), precisio...  32.6 us
    all_to_all x2, blocking collectives, regions_tell(): lax.all_to_all(jnp.stack([x0] * lax.axis_size('crs')), 'crs', 0, 0)  23.6 us
  transfers between devices with their start and end apart: 20, of which 10 were waited for; matrix products, arithmetic and copies ran while one was open for 0% of the time, Pallas kernels for 0%

profile of v1, /device:TPU:1, one launch (start us, length us, event | category | flops | bytes accessed | tf_op | source)
XLA Modules:
  0.0 998.4 jit_solution(7587649811188228826)
XLA Ops:
  9.5 1.5 collective-permute-start
  13.7 4.2 collective-permute-start.3
  20.6 2.9 fusion.30
  24.8 1.6 reduce_sum.81
  26.5 3.6 scatter_custom_fusion
  30.2 158.7 %all-reduce.5.cloned.1.call-done = f32[4,4096]{0,1:T(8,128)} async-done(((f32[4,4096]{0,1:T(8,128)}), f32[4,4096]{0,1:T(8,128)}) %all-reduce.5.cloned.1.call-update) | async-done | bytes 65552 | tf_op jit(solution)/shard_map/psum | solution.py:91
  188.9 10.9 %fusion.54 = f32[4,512]{1,0:T(4,128)S(1)} fusion(f32[4,4096]{0,1:T(8,128)} %all-reduce.5.cloned.1.call-done, f32[512,4096]{1,0:T(8,128)} %param.17), kind=kOutput, calls=%fused_computation.118 | convolution fusion | flops 100663296 | bytes 8462336 | tf_op jit(solution)/shard_map/dot_general | solution.py:92
  200.4 5.3 all-to-all-start
  206.0 6.5 all-to-all-done
  213.1 1.6 gather_fusion
  217.6 2.6 divide_add_fusion.2
  220.2 1.5 collective-permute-start.4
  223.4 4.0 collective-permute-start.7
  228.8 1.4 multiply_reduce_fusion.4
  230.2 71.2 %all-reduce = (f32[4]{0:T(128)}, f32[4]{0:T(128)}) all-reduce(f32[4]{0:T(128)} %get-tuple-element.4, f32[4]{0:T(128)S(1)} %get-tuple-element.3), channel_id=1, replica_groups=mesh['str'=16,'crs'=8] {'str','crs'}, use_global_device_ids=true, to_apply=%region_4.6 | all-reduce | flops 8 | bytes 64 | tf_op jit(solution)/shard_map/psum | solution.py:103
  302.1 2.8 multiply_subtract_fusion.2
  304.9 1.4 reshape.82
  306.8 3.6 scatter_custom_fusion.1
  310.7 147.2 %all-reduce.7.cloned.1.call-done = f32[4,4096]{0,1:T(8,128)} async-done(((f32[4,4096]{0,1:T(8,128)}), f32[4,4096]{0,1:T(8,128)}) %all-reduce.7.cloned.1.call-update) | async-done | bytes 65552 | tf_op jit(solution)/shard_map/psum | solution.py:91
  457.9 10.9 %fusion.55 = f32[4,512]{1,0:T(4,128)S(1)} fusion(f32[4,4096]{0,1:T(8,128)} %all-reduce.7.cloned.1.call-done, f32[512,4096]{1,0:T(8,128)} %param.17), kind=kOutput, calls=%fused_computation.119 | convolution fusion | flops 100663296 | bytes 8462336 | tf_op jit(solution)/shard_map/dot_general | solution.py:92
  468.8 11.8 %all_to_all.15 = f32[8,4,512]{2,1,0:T(4,128)S(1)} all-to-all(f32[8,4,512]{2,1,0:T(4,128)S(1)} %stack.7), channel_id=1, replica_groups=mesh['str'=16,'crs'=8] {'crs'}, dimensions={0} | all-to-all | bytes 131072 | tf_op jit(solution)/shard_map/all_to_all | solution.py:14
  480.6 2.0 copy.34
  482.6 3.3 gather_fusion.1
  485.9 1.8 broadcast_select_fusion.1
  490.3 2.4 reshape.85
  492.7 1.6 multiply_reduce_fusion.3
  494.2 63.6 %psum.67 = f32[4]{0:T(128)S(1)} all-reduce(f32[4]{0:T(128)S(1)} %multiply_reduce_fusion.3), channel_id=1, replica_groups=mesh['str'=16,'crs'=8] {'str','crs'}, use_global_device_ids=true, to_apply=%region_11.13 | all-reduce | flops 4 | bytes 32 | tf_op jit(solution)/shard_map/psum | solution.py:103
  557.9 1.9 multiply_add_fusion.2
  563.1 4.0 collective-permute-start.11
  571.0 71.4 %psum.68 = f32[4]{0:T(128)} all-reduce(f32[4]{0:T(128)} %multiply_reduce_fusion.2), channel_id=1, replica_groups=mesh['str'=16,'crs'=8] {'str','crs'}, use_global_device_ids=true, to_apply=%region_13.15 | all-reduce | flops 4 | bytes 32 | tf_op jit(solution)/shard_map/psum | solution.py:121
  643.6 3.1 multiply_subtract_fusion.1
  646.7 2.4 reshape.86
  649.0 1.6 reduce_sum.87
  651.5 4.0 scatter_custom_fusion.2
  655.5 147.2 %all-reduce.9.cloned.1.call-done = f32[4,4096]{0,1:T(8,128)} async-done(((f32[4,4096]{0,1:T(8,128)}), f32[4,4096]{0,1:T(8,128)}) %all-reduce.9.cloned.1.call-update) | async-done | bytes 65552 | tf_op jit(solution)/shard_map/psum | solution.py:91
  802.7 10.9 %fusion.56 = f32[4,512]{1,0:T(4,128)S(1)} fusion(f32[4,4096]{0,1:T(8,128)} %all-reduce.9.cloned.1.call-done, f32[512,4096]{1,0:T(8,128)} %param.17), kind=kOutput, calls=%fused_computation.120 | convolution fusion | flops 100663296 | bytes 8462336 | tf_op jit(solution)/shard_map/dot_general | solution.py:92
  813.6 11.8 %all_to_all.16 = f32[8,4,512]{2,1,0:T(4,128)S(1)} all-to-all(f32[8,4,512]{2,1,0:T(4,128)S(1)} %stack.8), channel_id=1, replica_groups=mesh['str'=16,'crs'=8] {'crs'}, dimensions={0} | all-to-all | bytes 131072 | tf_op jit(solution)/shard_map/all_to_all | solution.py:14
  825.4 2.0 copy.37
  827.4 3.2 gather_fusion.2
  830.6 1.8 broadcast_select_fusion
  834.9 2.4 reshape.89
  837.3 1.9 multiply_reduce_fusion.1
  839.2 63.8 %psum.70 = f32[4]{0:T(128)S(1)} all-reduce(f32[4]{0:T(128)S(1)} %multiply_reduce_fusion.1), channel_id=1, replica_groups=mesh['str'=16,'crs'=8] {'str','crs'}, use_global_device_ids=true, to_apply=%region_18.20 | all-reduce | flops 4 | bytes 32 | tf_op jit(solution)/shard_map/psum | solution.py:103
  903.0 1.9 multiply_add_fusion.1
  908.2 4.0 collective-permute-start.15
  915.6 70.9 %psum.71 = f32[4]{0:T(128)} all-reduce(f32[4]{0:T(128)S(1)} %multiply_reduce_fusion), channel_id=1, replica_groups=mesh['str'=16,'crs'=8] {'str','crs'}, use_global_device_ids=true, to_apply=%region_20.22 | all-reduce | flops 4 | bytes 32 | tf_op jit(solution)/shard_map/psum | solution.py:121
  987.2 2.7 multiply_add_fusion
  990.0 1.7 multiply_subtract_fusion
  (168 shorter events, 39.5 us)
Async XLA Ops:
  7.2 5.2 copy-start.1
  7.2 5.1 copy-start
  7.2 181.7 %all-reduce.5.cloned.1.call-start = ((), (), s32[]{:S(2)}) async-start(), calls=%async_computation.3 | async-start | bytes 4194304 | tf_op jit(solution)/shard_map/psum | solution.py:91
  8.1 9.8 copy-start.39
  8.1 9.8 copy-start.37
  9.5 10.4 %collective-permute-start = (f32[6,1,2048]{2,1,0:T(1,128)S(1)}, f32[6,1,2048]{2,1,0:T(1,128)S(1)}, u32[]{:S(2)}, u32[]{:S(2)}) collective-permute-start(f32[6,1,2048]{2,1,0:T(1,128)S(1)} %get-tuple-element.12), channel_id=1, source_target_pairs={{8,0},{16,8},{24,16},{32,24},{40,32},{48,40},{56,48},{64,56},{72,6... | collective-permute-start | bytes 147464 | tf_op jit(solution)/shard_map/ppermute | solution.py:31
  11.0 8.6 collective-permute-start.1
  12.4 7.1 collective-permute-start.2
  13.7 5.9 collective-permute-start.3
  19.8 3.7 copy-start.7
  19.8 3.7 copy-start.12
  19.8 3.7 copy-start.17
  23.5 6.7 copy-start.2
  23.5 3.0 copy-start.36
  30.2 175.7 %copy-start.38 = (s32[512]{0:T(512)S(1)}, s32[512]{0:T(512)}, u32[]{:S(2)}) copy-start(s32[512]{0:T(512)} %compare_select_fusion) | copy-start | bytes 6148
  200.4 12.0 %all-to-all-start = ((f32[8,4,512]{2,1,0:T(4,128)}), f32[8,4,512]{2,1,0:T(4,128)S(1)}, u32[]{:S(2)}, u32[]{:S(2)}) async-start(f32[8,4,512]{2,1,0:T(4,128)} %stack.6), calls=%async_computation | async-start | bytes 131072 | tf_op jit(solution)/shard_map/all_to_all | solution.py:14
  205.7 252.2 %all-reduce.7.cloned.1.call-start = ((), (), s32[]{:S(2)}) async-start(), calls=%async_computation.4 | async-start | bytes 4194304 | tf_op jit(solution)/shard_map/psum | solution.py:91
  217.6 11.1 %copy-start.3 = (f32[4,32,2048]{2,1,0:T(8,128)S(1)}, f32[4,32,2048]{2,1,0:T(8,128)}, u32[]{:S(2)}) copy-start(f32[4,32,2048]{2,1,0:T(8,128)} %copy-done.2) | copy-start | bytes 3145732
  217.6 11.2 %copy-start.8 = (f32[32,2048]{1,0:T(8,128)S(1)}, f32[32,2048]{1,0:T(8,128)}, u32[]{:S(2)}) copy-start(f32[32,2048]{1,0:T(8,128)} %copy-done.7) | copy-start | bytes 786436
  217.6 11.2 %copy-start.13 = (f32[32,2048]{1,0:T(8,128)S(1)}, f32[32,2048]{1,0:T(8,128)}, u32[]{:S(2)}) copy-start(f32[32,2048]{1,0:T(8,128)} %copy-done.12) | copy-start | bytes 786436
  217.6 11.2 %copy-start.18 = (f32[32,2048]{1,0:T(8,128)S(1)}, f32[32,2048]{1,0:T(8,128)}, u32[]{:S(2)}) copy-start(f32[32,2048]{1,0:T(8,128)} %copy-done.17) | copy-start | bytes 786436
  220.2 8.5 collective-permute-start.4
  221.7 7.0 collective-permute-start.5
  222.1 5.4 collective-permute-start.6
  223.4 5.3 collective-permute-start.7
  228.8 73.3 %copy-start.4 = (f32[4,32,2048]{2,1,0:T(8,128)S(1)}, f32[4,32,2048]{2,1,0:T(8,128)}, u32[]{:S(2)}) copy-start(f32[4,32,2048]{2,1,0:T(8,128)} %copy-done.2) | copy-start | bytes 3145732
  310.4 492.2 %all-reduce.9.cloned.1.call-start = ((), (), s32[]{:S(2)}) async-start(), calls=%async_computation.5 | async-start | bytes 4194304 | tf_op jit(solution)/shard_map/psum | solution.py:91
  482.6 10.0 %copy-start.6 = (f32[4,32,2048]{2,1,0:T(8,128)S(1)}, f32[4,32,2048]{2,1,0:T(8,128)}, u32[]{:S(2)}) copy-start(f32[4,32,2048]{2,1,0:T(8,128)} %multiply_subtract_fusion.2) | copy-start | bytes 3145732
  492.7 65.2 %copy-start.44 = (f32[4]{0:T(128)S(1)}, f32[4]{0:T(128)}, u32[]{:S(2)}) copy-start(f32[4]{0:T(128)} %get-tuple-element.5) | copy-start | bytes 52
  557.9 11.8 %copy-start.9 = (f32[32,2048]{1,0:T(8,128)S(1)}, f32[32,2048]{1,0:T(8,128)}, u32[]{:S(2)}) copy-start(f32[32,2048]{1,0:T(8,128)} %copy-done.7) | copy-start | bytes 786436
  557.9 11.8 %copy-start.14 = (f32[32,2048]{1,0:T(8,128)S(1)}, f32[32,2048]{1,0:T(8,128)}, u32[]{:S(2)}) copy-start(f32[32,2048]{1,0:T(8,128)} %copy-done.12) | copy-start | bytes 786436
  557.9 11.8 %copy-start.19 = (f32[32,2048]{1,0:T(8,128)S(1)}, f32[32,2048]{1,0:T(8,128)}, u32[]{:S(2)}) copy-start(f32[32,2048]{1,0:T(8,128)} %copy-done.17) | copy-start | bytes 786436
  559.9 8.5 collective-permute-start.8
  560.9 7.5 collective-permute-start.9
  561.8 5.7 collective-permute-start.10
  563.1 5.3 collective-permute-start.11
  837.3 65.7 %copy-start.43 = (f32[4]{0:T(128)S(1)}, f32[4]{0:T(128)}, u32[]{:S(2)}) copy-start(f32[4]{0:T(128)} %copy-done.42) | copy-start | bytes 52
  903.0 11.8 %copy-start.10 = (f32[32,2048]{1,0:T(8,128)S(1)}, f32[32,2048]{1,0:T(8,128)}, u32[]{:S(2)}) copy-start(f32[32,2048]{1,0:T(8,128)} %copy-done.7) | copy-start | bytes 786436
  903.0 11.8 %copy-start.15 = (f32[32,2048]{1,0:T(8,128)S(1)}, f32[32,2048]{1,0:T(8,128)}, u32[]{:S(2)}) copy-start(f32[32,2048]{1,0:T(8,128)} %copy-done.12) | copy-start | bytes 786436
  903.0 11.8 %copy-start.20 = (f32[32,2048]{1,0:T(8,128)S(1)}, f32[32,2048]{1,0:T(8,128)}, u32[]{:S(2)}) copy-start(f32[32,2048]{1,0:T(8,128)} %copy-done.17) | copy-start | bytes 786436
  905.0 8.6 copy-start.22
  905.0 82.2 %copy-start.41 = (f32[4]{0:T(128)S(1)}, f32[4]{0:T(128)}, u32[]{:S(2)}) copy-start(f32[4]{0:T(128)} %copy-done.40) | copy-start | bytes 52
  905.0 8.5 collective-permute-start.12
  906.0 7.5 collective-permute-start.13
  906.9 5.7 collective-permute-start.14
  908.2 5.3 collective-permute-start.15
  987.2 2.7 copy-start.5
  987.2 2.7 copy-start.11
  (17 other events, 24.5 us)
Sparse Core Ops, SparseCore 0:
  30.3 158.5 all-reduce.4
  310.6 147.3 all-reduce.6
  655.6 146.9 all-reduce.8
